TPU v7x, 32 devices: a whole 2x2x4 slice. The times are simulated.
32 devices in a mesh: fld: 4 (over z), wn: 8 (over y, x, core).
Axes of the slice: x: 2, y: 2, z: 4, core: 2. Of those that a mesh axis runs over, the one named last changes fastest.
Arguments:
- spec_tq: bfloat16 [640, 2, 16, 2, 1281], P('wn', None, 'fld'), may hold values from -0.119628906 to 0.119628906
- spec_sp: bfloat16 [640, 2, 1281], P('wn'), may hold values from -0.119628906 to 0.119628906
- legendre: bfloat16 [640, 128, 1281], P('wn'), may hold values from -0.15625 to 0.15625
- low_wavenumber: int32 [640], replicated, may hold values from 0 to 639, each once
- lon_points: int32 [128], replicated, may hold values from 20 to 5136, as said below
- requested_elevation: int32 [256, 5632], P('wn', 'fld'), may hold values from 30 to 1599
Outputs:
- temperature_anomaly: float32 [256, 5632], P('wn', 'fld')
- humidity_ratio: float32 [256, 5632], P('wn', 'fld')
Inputs may be any that keep to these rules, and one draw needn't show every extreme that they name: `low_wavenumber`: every number 0 to 639 is the lower wavenumber of exactly one pair. `lon_points`: row entries are 4 j + 16 for octahedral row numbers j between 1 and 1280, not decreasing along the rows; the first row has 20 points and the last row 5136.
All inputs are finite; a program needn't handle non-finite values.
Results may differ from a plain program's by a relative error of at most 0.0037.
Values sent between devices are 32-bit elements; how exact they have to be, the bound alone decides.
No kernel may reach another device: no remote copies, remote signals or barrier semaphores. Data moves between devices by JAX's collectives and lax.ppermute only.
A program may use at most 192 MiB of HBM per device.

v0:
```python
import math

import jax
import jax.numpy as jnp
from jax import lax
from jax.sharding import PartitionSpec as P

group_width = 128
thickness_scale = 0.012 * 287.05 / 9.80665
log_step = 0.012


def wave_table(wave_line, points, group_ids):
    residue = wave_line[:, None] * (group_ids[None, :] * group_width) % points
    phase = residue.astype(jnp.float32) * (2.0 * math.pi / points.astype(jnp.float32))
    return jnp.concatenate([jnp.cos(phase), -jnp.sin(phase)], 0).astype(jnp.bfloat16)


def twisted(coeffs, wave_line, points):
    lanes = jnp.arange(group_width, dtype=jnp.int32)
    residue = lanes[:, None] * wave_line[None, :] % points
    phase = residue.astype(jnp.float32) * (2.0 * math.pi / points.astype(jnp.float32))
    cosine = jnp.cos(phase)[:, None, :]
    sine_part = jnp.sin(phase)[:, None, :]
    weight = jnp.where(wave_line == 0, jnp.float32(1.0), jnp.float32(2.0)) * (
        2 * wave_line < points
    ).astype(jnp.float32)
    real_part = coeffs[None, :, 0, :]
    imag_part = coeffs[None, :, 1, :]
    turned_re = weight * (real_part * cosine - imag_part * sine_part)
    turned_im = weight * (real_part * sine_part + imag_part * cosine)
    return jnp.concatenate([turned_re, turned_im], 2).astype(jnp.bfloat16)


def contract(coeffs, wave_line, points, group_ids):
    return jnp.einsum(
        "qfj,jp->fpq",
        twisted(coeffs, wave_line, points),
        wave_table(wave_line, points, group_ids),
        preferred_element_type=jnp.float32,
    )


def synthesize(coeffs, wave_line, points, group_ids):
    summed = contract(coeffs, wave_line, points, group_ids)
    return summed.reshape(coeffs.shape[0], -1)


def synthesize_rows(coeffs, wave_line, grid_point_rows, group_ids):

    def one_row(row_args):
        return synthesize(row_args[0], wave_line, row_args[1], group_ids)

    result = lax.map(one_row, (coeffs, grid_point_rows))
    longitude = (
        group_ids[:, None] * group_width + jnp.arange(group_width, dtype=jnp.int32)[None, :]
    ).reshape(-1)
    return jnp.where(
        longitude[None, None, :] < grid_point_rows[:, None, None], result, jnp.float32(0.0)
    )


def estimate_column(kelvin_by_stratum, moisture_by_stratum, bottom_boundary, elevation_array):
    kelvin_field = 288.0 + 12.0 * kelvin_by_stratum
    water_vapour_share = 0.008 + 0.002 * moisture_by_stratum
    density_weighted_kelvin = kelvin_field * (1.0 + 0.608 * water_vapour_share)
    stratum_average = jnp.concatenate(
        [
            density_weighted_kelvin[:1],
            0.5 * (density_weighted_kelvin[1:] + density_weighted_kelvin[:-1]),
        ],
        0,
    )
    heights_lev = jnp.cumsum(thickness_scale * stratum_average, axis=0)
    mixing_weight = jnp.clip(
        (elevation_array[None] - heights_lev[:-1]) / (heights_lev[1:] - heights_lev[:-1]), 0.0, 1.0
    )
    kelvin_interpolated = kelvin_field[0] + jnp.sum(
        mixing_weight * (kelvin_field[1:] - kelvin_field[:-1]), 0
    )
    moisture_interpolated = water_vapour_share[0] + jnp.sum(
        mixing_weight * (water_vapour_share[1:] - water_vapour_share[:-1]), 0
    )
    logarithmic_barometric = (
        math.log(100000.0) + 0.15 * bottom_boundary - log_step * (1.0 + jnp.sum(mixing_weight, 0))
    )
    vapour_maximum = 611.2 * jnp.exp(
        17.67 * (kelvin_interpolated - 273.15) / (kelvin_interpolated - 29.65)
    )
    return (
        (kelvin_interpolated - 288.0) / 12.0,
        moisture_interpolated * jnp.exp(logarithmic_barometric) / (0.622 * vapour_maximum),
    )


def shards(spec_tq, spec_sp, legendre, low_wavenumber, lon_points, requested_elevation):
    wn_count = lax.axis_size("wn")
    fld_count = lax.axis_size("fld")
    pair_dev = spec_tq.shape[0]
    lev_dev = spec_tq.shape[2]
    packed = spec_tq.shape[4]
    wave_count = packed - 1
    half_rows = legendre.shape[1]
    all_rows = 2 * half_rows
    band_rows = all_rows // wn_count
    tile_width = requested_elevation.shape[1]
    wn_index = lax.axis_index("wn")
    fld_index = lax.axis_index("fld")
    low_local = lax.dynamic_slice_in_dim(low_wavenumber, wn_index * pair_dev, pair_dev)
    position = jnp.arange(packed, dtype=jnp.int32)[None, :]
    boundary = (wave_count - low_local)[:, None]
    higher = position >= boundary
    odd_degree = jnp.where(higher, position - boundary, position) % 2 == 1
    selectors = jnp.stack(
        [~higher & ~odd_degree, ~higher & odd_degree, higher & ~odd_degree, higher & odd_degree], 1
    )
    spectra = jnp.concatenate([spec_tq.reshape(pair_dev, 4 * lev_dev, packed), spec_sp], 1)
    selected = jnp.where(
        selectors[:, :, None, :], spectra[:, None, :, :], jnp.zeros((), jnp.bfloat16)
    )
    partial_sums = jnp.einsum(
        "prk,pjck->prjc", legendre, selected, preferred_element_type=jnp.float32
    )
    northern = partial_sums[:, :, 0::2] + partial_sums[:, :, 1::2]
    southern = partial_sums[:, :, 0::2] - partial_sums[:, :, 1::2]
    merged = jnp.concatenate([northern, southern[:, ::-1]], 1)
    channels = spectra.shape[1]
    fourier = jnp.transpose(merged, (1, 3, 0, 2)).reshape(all_rows, channels, 2 * pair_dev)
    ordinal = jnp.arange(band_rows, dtype=jnp.int32)
    my_rows = wn_index * band_rows + ordinal
    exchanged = lax.all_to_all(fourier, "wn", split_axis=0, concat_axis=2, tiled=True)
    coeffs = exchanged.reshape(band_rows, channels // 2, 2, wave_count)
    field_count = coeffs.shape[1]
    slot_index = jnp.arange(wave_count, dtype=jnp.int32)
    pair_low = low_wavenumber[slot_index // 2]
    wave_line = jnp.where(slot_index % 2 == 0, pair_low, wave_count - 1 - pair_low)
    row_ids = jnp.where(my_rows < half_rows, my_rows, all_rows - 1 - my_rows)
    grid_point_rows = lon_points[row_ids]
    tile_groups = tile_width // group_width
    physical_space_data = synthesize_rows(
        coeffs, wave_line, grid_point_rows, jnp.arange(tile_groups * fld_count, dtype=jnp.int32)
    )
    bottom_boundary = lax.dynamic_slice_in_dim(
        physical_space_data[:, field_count - 1], fld_index * tile_width, tile_width, 1
    )
    columns = lax.all_to_all(
        physical_space_data[:, : field_count - 1], "fld", split_axis=2, concat_axis=1, tiled=True
    )
    levels = columns.reshape(band_rows, fld_count, 2, lev_dev, tile_width)
    levels = jnp.transpose(levels, (2, 1, 3, 0, 4)).reshape(
        2, fld_count * lev_dev, band_rows, tile_width
    )
    kelvin_result, mixing_ratio_result = estimate_column(
        levels[0], levels[1], bottom_boundary, requested_elevation.astype(jnp.float32)
    )
    longitude = fld_index * tile_width + jnp.arange(tile_width, dtype=jnp.int32)
    inside = longitude[None, :] < grid_point_rows[:, None]
    kelvin_result = jnp.where(inside, kelvin_result, jnp.float32(0.0))
    mixing_ratio_result = jnp.where(inside, mixing_ratio_result, jnp.float32(0.0))
    return (kelvin_result, mixing_ratio_result)


def solution(mesh):
    in_specs = (
        P("wn", None, "fld", None, None),
        P("wn", None, None),
        P("wn", None, None),
        P(),
        P(),
        P("wn", "fld"),
    )
    out_specs = (P("wn", "fld"), P("wn", "fld"))
    return jax.shard_map(shards, mesh=mesh, in_specs=in_specs, out_specs=out_specs, check_vma=False)
```

profile of v0, /device:TPU:0, one launch (start us, length us, event | category | flops | bytes accessed | tf_op | source)
XLA Modules:
  0.0 1164.7 jit_solution(9052810482297039425)
XLA Ops:
  5.3 8.6 reshape.455
  18.9 23.5 %fusion.44 = f32[80,128,4,18]{1,3,2,0:T(8,128)S(1)} fusion(bf16[80,128,1281,1]{1,0,2,3:T(8,128)(2,1)} %bitcast.91, pred[80,4,1281]{2,1,0:T(4,128)(4,1)S(1)} %pad_add_fusion, bf16[80,18,1281]{2,1,0:T(8,128)(2,1)S(1)} %pad_maximum_fusion), kind=kOutput, calls=%fused_computation.70 | convolution fusion | flops 1896289920 | bytes 33283200 | tf_op jit(solution)/shard_map/prk,pjck->prjc/dot_general | solution.py:121
  50.9 6.6 copy.27
  57.6 9.3 reshape.478
  79.2 29.1 %all-to-all-done = f32[8,1,92160]{2,1,0:T(1,128)S(1)} async-done(((f32[8,1,92160]{2,1,0:T(1,128)}), f32[8,1,92160]{2,1,0:T(1,128)S(1)}, u32[]{:S(2)}, u32[]{:S(2)}) %all-to-all-start) | async-done | bytes 2949152 | tf_op jit(solution)/shard_map/all_to_all | solution.py:131
  108.7 10.2 reduce.2
  119.0 7.8 reshape.479
  126.8 7.6 copy.29
  138.6 781.7 %while.12 = (s32[]{:T(128)}, f32[32,9,5632]{2,0,1:T(8,128)}, s32[1280]{0:T(1024)S(1)}, s32[32]{0:T(128)S(1)}, f32[32,9,2,1280]{3,0,2,1:T(8,128)S(1)}) while((s32[]{:T(128)}, f32[32,9,5632]{2,0,1:T(8,128)}, s32[1280]{0:T(1024)S(1)}, s32[32]{0:T(128)S(1)}, f32[32,9,2,1280]{3,0,2,1:T(8,128)S(1)}) %tuple.56), condition=%wide.region_1.2_spmd.clone.clone, body=%wide.region_0.1_spmd.clone.sunk.clone | while | flops 288892224 | bytes 16553474 | solution.py:54
  155.2 8.6 fusion.75
  179.4 8.6 fusion.75
  203.5 8.6 fusion.75
  227.6 8.6 fusion.75
  251.8 8.6 fusion.75
  275.9 8.6 fusion.75
  300.1 8.6 fusion.75
  324.2 8.6 fusion.75
  348.4 8.6 fusion.75
  372.5 8.6 fusion.75
  396.6 8.6 fusion.75
  420.7 8.6 fusion.75
  444.8 8.6 fusion.75
  469.0 8.6 fusion.75
  493.1 8.6 fusion.75
  517.2 8.6 fusion.75
  541.3 8.6 fusion.75
  565.4 8.6 fusion.75
  589.5 8.6 fusion.75
  613.7 8.6 fusion.75
  637.8 8.6 fusion.75
  661.9 8.6 fusion.75
  686.0 8.6 fusion.75
  710.1 8.6 fusion.75
  734.3 8.6 fusion.75
  758.4 8.6 fusion.75
  782.5 8.6 fusion.75
  806.6 8.6 fusion.75
  830.7 8.6 fusion.75
  854.9 8.6 fusion.75
  879.0 8.6 fusion.75
  903.1 8.6 fusion.75
  929.4 14.0 %copy.33 = f32[32,8,5632]{0,1,2:T(8,128)} copy(f32[32,8,5632]{2,0,1:T(8,128)} %slice.87) | data formatting | bytes 11534336 | tf_op jit(solution)/shard_map/slice | solution.py:147
  943.4 25.0 %reshape.480 = f32[4,1,360448]{2,1,0:T(1,128)} reshape(f32[5632,8,32]{2,1,0:T(8,128)} %bitcast.80) | data formatting | bytes 11534336
  973.8 124.3 %all-to-all-done.1 = f32[4,1,360448]{2,1,0:T(1,128)} async-done(((f32[4,1,360448]{2,1,0:T(1,128)}), f32[4,1,360448]{2,1,0:T(1,128)}, u32[]{:S(2)}, u32[]{:S(2)}) %all-to-all-start.1) | async-done | bytes 5767200 | tf_op jit(solution)/shard_map/all_to_all | solution.py:146
  1098.2 20.4 %reduce.3 = f32[4,360448]{1,0:T(4,128)} reduce(f32[4,1,360448]{2,1,0:T(1,128)} %all-to-all-done.1, f32[]{:T(128)} %broadcast.546), dimensions={1}, to_apply=%all_to_all.25.reduce_sub_computation | reduce | bytes 11534340 | tf_op jit(solution)/shard_map/all_to_all | solution.py:146
  1118.6 18.3 %reshape.481 = f32[5632,8,32]{2,1,0:T(8,128)} reshape(f32[4,360448]{1,0:T(4,128)} %reduce.3) | data formatting | bytes 11534336
  1136.8 16.4 %copy.40 = f32[32,8,4,1408]{3,2,1,0:T(4,128)} copy(f32[32,8,4,1408]{0,1,3,2:T(8,128)} %bitcast.81) | data formatting | bytes 11534336 | tf_op jit(solution)/shard_map/all_to_all | solution.py:146
  1153.3 6.0 copy.35
  (399 shorter events, 480.4 us)
Async XLA Ops:
  0.6 76.9 %copy-start = (s32[128]{0:T(128)S(1)}, s32[128]{0:T(128)}, u32[]{:S(2)}) copy-start(s32[128]{0:T(128)} %param.12) | copy-start | bytes 1540
  5.3 8.6 copy-start.4
  66.9 5.6 copy-start.2
  66.9 41.3 %all-to-all-start = ((f32[8,1,92160]{2,1,0:T(1,128)}), f32[8,1,92160]{2,1,0:T(1,128)S(1)}, u32[]{:S(2)}, u32[]{:S(2)}) async-start(f32[8,1,92160]{2,1,0:T(1,128)} %reshape.478), calls=%async_computation | async-start | bytes 5898240 | tf_op jit(solution)/shard_map/all_to_all | solution.py:131
  923.9 2.7 copy-start.3
  968.5 5.3 copy-start.5
  968.5 129.7 %all-to-all-start.1 = ((f32[4,1,360448]{2,1,0:T(1,128)}), f32[4,1,360448]{2,1,0:T(1,128)}, u32[]{:S(2)}, u32[]{:S(2)}) async-start(f32[4,1,360448]{2,1,0:T(1,128)} %reshape.480), calls=%async_computation.1 | async-start | bytes 11534336 | tf_op jit(solution)/shard_map/all_to_all | solution.py:146
  1161.4 1.9 slice-start
  1161.4 2.8 copy-start.1
where the time goes:
time: 1180 us; the launch traced here: 1160 us
  other arithmetic  528 us (45%)
  local copies, waits for them, and re-layouts  310 us (26%)
  waiting for transfers between devices  153 us (13%)
  matrix products  81.2 us (7%)
  loops' own time  80.2 us (7%)
    cos x32, other arithmetic, twisted(): cosine = jnp.cos(phase)[:, None, :]  276 us
    another operation x64, other arithmetic  174 us
    dynamic_update_slice x32, local copies, waits for them, and re-layouts, synthesize_rows(): result = lax.map(one_row, (coeffs, grid_point_rows))  141 us
    all_to_all x1, waiting for transfers between devices, shards(): lax.all_to_all(physical_space_data[:, :field_count - 1], 'fld', split_axi...  124 us
    another operation x1, loops' own time, synthesize_rows(): result = lax.map(one_row, (coeffs, grid_point_rows))  80.2 us
    unnamed x16, local copies, waits for them, and re-layouts  63.1 us
    dot_general x32, matrix products, contract(): jnp.einsum('qfj,jp->fpq', twisted(coeffs, wave_line, points), wave_table(...  57.7 us
    all_to_all x1, waiting for transfers between devices, shards(): lax.all_to_all(fourier, 'wn', split_axis=0, concat_axis=2, tiled=True)  29.1 us
  transfers between devices with their start and end apart: 2, of which 2 were waited for; matrix products, arithmetic and copies ran while one was open for 1% of the time, Pallas kernels for 0%

commit v1 on v0

v1 whole, which is shorter than its diff:
```python
import functools
import math

import jax
import jax.numpy as jnp
from jax import lax
from jax.experimental import pallas as pl
from jax.experimental.pallas import tpu as pltpu
from jax.sharding import PartitionSpec as P

lanes = 128
depth = 256
channel_rows = 16
near, far = 3, 25
thickness_scale = 0.012 * 287.05 / 9.80665
log_step = 0.012


def tile_of(t, g, fld_count):
    return t * fld_count + (g if t % 2 == 0 else fld_count - 1 - g)


def turned_over(rows):
    high = rows.astype(jnp.bfloat16)
    low = (rows - high.astype(jnp.float32)).astype(jnp.bfloat16)
    row = lax.broadcasted_iota(jnp.int32, (lanes, 2 * lanes), 0)
    column = lax.broadcasted_iota(jnp.int32, (lanes, 2 * lanes), 1)
    unit = (row == (column & (lanes - 1))).astype(jnp.float32).astype(jnp.bfloat16)
    return lax.dot_general(
        unit, jnp.concatenate([high, low], 1), (((1,), (1,)), ((), ())),
        preferred_element_type=jnp.float32,
    )


def legendre_kernel(
    sizes, low_ref, spec_ref, sp_ref, plane_ref, elevation_ref, known_ref, *rest
):
    fld_count, wn_count, pair_dev, group, last, levels, halves, turns, head, starts, pitches = sizes
    out_count = len(pitches) + (1 if head else 0)
    (*out_refs, matrix, total, even_rows, odd_rows, stage) = rest[: out_count + 5]
    sp_rows = out_refs.pop() if head else rest[-1]
    first_block = 0 if head else 1
    out_of = [0 if head else n for n in range(turns // 2)]
    half, step = pl.program_id(0), pl.program_id(1)
    block = step + first_block
    own, own_wn = lax.axis_index("fld"), lax.axis_index("wn")
    packed = last + 1
    channels = 4 * levels
    main_rows = 4 * channel_rows
    dest = fld_count * wn_count
    tiles = lanes // wn_count
    share = pair_dev // fld_count
    position = lax.broadcasted_iota(jnp.int32, (channel_rows, packed), 1)
    alternate = (1 - 2 * (position & 1)).astype(jnp.float32).astype(jnp.bfloat16)

    def build(i):
        pair = block * group + i
        low = low_ref[own_wn * pair_dev + pair]
        low_odd = (low & 1).astype(jnp.float32)
        below = position < last - low
        first = jnp.where(below, 1.0 - low_odd, low_odd).astype(jnp.bfloat16)
        flip = (1.0 - 2.0 * low_odd).astype(jnp.bfloat16)
        values = spec_ref[i].reshape(channels, packed)
        if channels < channel_rows:
            filler = jnp.zeros((channel_rows - channels, packed), jnp.bfloat16)
            values = jnp.concatenate([values, filler], 0)

        def four(values, first, alternate):
            swung = values * alternate
            even, even_swung = values * first, swung * first
            return even, even_swung * flip, values - even, swung - even_swung

        for n, rows in enumerate(four(values, first, alternate)):
            matrix[i, n * channel_rows : (n + 1) * channel_rows, :packed] = rows

        @pl.when((pair >= own * share) & (pair < (own + 1) * share))
        def _():
            pressure = sp_ref[i].astype(jnp.float32)
            single = first[:1].astype(jnp.float32)
            sign = alternate[:1].astype(jnp.float32)
            even, swung = pressure * single, pressure * sign
            even_swung = swung * single
            rows = [even, even_swung * flip.astype(jnp.float32), pressure - even, swung - even_swung]
            matrix[i, main_rows:, :packed] = jnp.concatenate(rows * 2, 0).astype(jnp.bfloat16)

    @pl.loop(0, group // 2)
    def _(n):
        build(2 * n)
        build(2 * n + 1)

    chunks = last // depth
    pitch = group + 1

    def widen(begin, end, buffer):
        for k in range(begin, end):
            rows = plane_ref[k].astype(jnp.float32)
            for n in range(group // 8):
                at = n * depth * far + (k % depth) * far
                buffer[pl.ds(at, 8, stride=near), :] = rows[8 * n : 8 * n + 8]

    buffers = (even_rows, odd_rows)
    widen(0, depth, buffers[0])
    for chunk in range(chunks):
        source, target = buffers[chunk % 2], buffers[(chunk + 1) % 2]
        for i in range(group):
            at = (i // 8) * depth * far + (i % 8) * near
            plane = source[pl.ds(at, depth, stride=far), :].astype(jnp.bfloat16)
            part = jnp.dot(
                matrix[i, :, chunk * depth : (chunk + 1) * depth],
                plane,
                preferred_element_type=jnp.float32,
            )
            if chunk == 0:
                total[i] = part
            else:
                total[i] += part
            if chunk + 1 < chunks:
                begin = (chunk + 1) * depth
                widen(begin + depth * i // group, begin + depth * (i + 1) // group, target)

    tail = plane_ref[last].astype(jnp.float32)
    low_lanes = lax.broadcasted_iota(jnp.int32, (wn_count, lanes), 1) < lanes // 2
    for first in range(0, group, 4):
        four = []
        for j in range(first, first + 4):
            column = matrix[j, :, last : last + 1].astype(jnp.float32)
            summed = total[j] + column * tail[j : j + 1]
            four.append(summed[:main_rows])
            at = ((half if head else block) * group + j) * 8
            sp_rows[pl.ds(pl.multiple_of(at, 8), 8), :] = summed[main_rows : main_rows + 8]
        quad = turned_over(jnp.concatenate(four, 0))
        for i in (first, first + 2):
            turned = quad[:, (i - first) * lanes // 2 :][:, :lanes]
            here = [turned[b * wn_count : (b + 1) * wn_count] for b in range(tiles)]
            moved = [pltpu.roll(tile, lanes // 2, 1) for tile in here]
            for n in range(turns // 2):
                for g in range(fld_count):
                    if halves == 1:
                        b, c = tile_of(2 * n, g, fld_count), tile_of(2 * n + 1, g, fld_count)
                        both = (
                            jnp.where(low_lanes, here[b], moved[c]),
                            jnp.where(low_lanes, moved[b], here[c]),
                        )
                    else:
                        c = fld_count - 1 - g
                        both = (
                            jnp.where(half == 0, here[g], moved[c]),
                            jnp.where(half == 0, moved[g], here[c]),
                        )
                    for j in range(2):
                        at = g * wn_count * pitch + i + j
                        stage[n, pl.ds(at, wn_count, stride=pitch), :] = both[j]

    for n in range(turns // 2):
        out = out_refs[out_of[n]]
        for d in range(dest):
            rows = stage[n, d * pitch : d * pitch + group, :]
            at = d * pitches[out_of[n]] + starts[n] + step * group
            at = pl.ds(pl.multiple_of(at, 8), group)
            if halves > 1:
                lane = lax.broadcasted_iota(jnp.int32, (group, lanes), 1)
                rows = jnp.where((lane < lanes // 2) & (half == 1), out[at, :], rows)
            out[at, :] = rows

    if head:
        slabs = elevation_ref.shape[1] // lanes
        band_rows = elevation_ref.shape[0]
        band_tiles = band_rows // wn_count

        @pl.when((half == 0) & (step == 0))
        def _():
            north = own_wn < wn_count // 2
            band = jnp.where(north, own_wn, wn_count - 1 - own_wn)
            turn = band * band_tiles // fld_count
            for d in range(dest):
                g, e = d // wn_count, d % wn_count
                tile = jnp.where(turn % 2 == 0, g, fld_count - 1 - g)
                inside = jnp.clip(turn * fld_count + tile - band * band_tiles, 0, band_tiles - 1)
                row = inside * wn_count + e
                row = jnp.where(north, row, band_rows - 1 - row)
                heights = elevation_ref[pl.ds(row, 1), :].astype(jnp.float32)
                for n in range(slabs):
                    at = d * pitches[0] + turns // 2 * group + n
                    out_refs[0][at : at + 1, :] = heights[:, n * lanes : (n + 1) * lanes]

        return

    @pl.when(step == 0)
    def _():
        sp_rows[: group * 8, :] = known_ref[pl.ds(pl.multiple_of(half * group * 8, 8), group * 8), :]

    out, row_pitch, carried = out_refs[-1], pitches[-1], pair_dev - group

    @pl.when(block == pair_dev // group - 1)
    def _():
        spot = lax.broadcasted_iota(jnp.int32, (wn_count, lanes), 1) // 32
        for n in range(-(-share // 4)):
            rows = sp_rows[pl.ds(pl.multiple_of((own * share + 4 * n) * 8, 8), 32), :]
            turned = turned_over(jnp.concatenate([rows] * 4, 0))
            here = [turned[b * wn_count : (b + 1) * wn_count] for b in range(tiles)]
            for g in range(fld_count):
                at = pl.ds(g * wn_count * row_pitch + carried + n, wn_count, stride=row_pitch)
                if halves == 1:
                    value = here[tile_of(turns - 1, g, fld_count)]
                    for t in range(turns - 1):
                        value = jnp.where(spot == t, here[tile_of(t, g, fld_count)], value)
                else:
                    value = jnp.where(half == 0, here[g], here[fld_count - 1 - g])
                    value = jnp.where((spot == 0) & (half == 1), out[at, :], value)
                out[at, :] = value


def legendre_sums(
    spec_tq, spec_sp, legendre, low_wavenumber, elevation, fld_count, wn_count, group, known
):
    pair_dev, _, levels, _, packed = spec_tq.shape
    half_rows = legendre.shape[1]
    last = packed - 1
    head = known is None
    turns = half_rows // (wn_count * fld_count)
    halves = half_rows // lanes
    planes = jnp.transpose(legendre, (2, 0, 1))
    dest = fld_count * wn_count
    rows = 4 * channel_rows + 16
    width = -(-packed // lanes) * lanes
    if head:
        starts, first_block, blocks = [n * group for n in range(turns // 2)], 0, 1
        slabs = elevation.shape[1] // lanes
        pitches = [-(-(group * turns // 2 + slabs) // 8) * 8]
        known = jnp.zeros((8, lanes), jnp.float32)
    else:
        starts, first_block, blocks = [0] * (turns // 2), 1, pair_dev // group - 1
        extra = -(-(pair_dev // fld_count) // 4)
        pitches = [pair_dev - group] * (turns // 2)
        pitches[-1] += -(-extra // 8) * 8
    sizes = (
        fld_count, wn_count, pair_dev, group, last, levels, halves, turns, head, tuple(starts), tuple(pitches)
    )
    shapes = [(dest * pitch, lanes) for pitch in pitches]
    outs = shapes + ([(halves * group * 8, lanes)] if head else [])
    work = blocks * group * (rows * last * lanes * 2) * halves
    out = pl.pallas_call(
        functools.partial(legendre_kernel, sizes),
        grid_spec=pltpu.PrefetchScalarGridSpec(
            num_scalar_prefetch=1,
            grid=(halves, blocks),
            in_specs=[
                pl.BlockSpec(
                    (group, 2, levels, 2, packed), lambda h, b, *_: (b + first_block, 0, 0, 0, 0)
                ),
                pl.BlockSpec((group, 2, packed), lambda h, b, *_: (b + first_block, 0, 0)),
                pl.BlockSpec((packed, group, lanes), lambda h, b, *_: (0, b + first_block, h)),
                pl.BlockSpec(elevation.shape, lambda h, b, *_: (0, 0)),
                pl.BlockSpec(known.shape, lambda h, b, *_: (0, 0)),
            ],
            out_specs=[pl.BlockSpec(shape, lambda h, b, *_: (0, 0)) for shape in outs],
            scratch_shapes=[
                pltpu.VMEM((group, rows, width), jnp.bfloat16),
                pltpu.VMEM((group, rows, lanes), jnp.float32),
                pltpu.VMEM((group // 8 * depth * far, lanes), jnp.float32),
                pltpu.VMEM((group // 8 * depth * far, lanes), jnp.float32),
                pltpu.VMEM((turns // 2, dest * (group + 1), lanes), jnp.float32),
            ]
            + ([] if head else [pltpu.VMEM((pair_dev * 8 + 32, lanes), jnp.float32)]),
        ),
        out_shape=[jax.ShapeDtypeStruct(shape, jnp.float32) for shape in outs],
        compiler_params=pltpu.CompilerParams(vmem_limit_bytes=56 * 1024 * 1024),
        cost_estimate=pl.CostEstimate(
            flops=work, bytes_accessed=blocks * group * packed * lanes * 2 * halves, transcendentals=0
        ),
        name="legendre_head" if head else "legendre_rest",
    )(low_wavenumber, spec_tq, spec_sp, planes, elevation, known)
    return [block.reshape(dest, -1, lanes) for block in out[: len(pitches)]] + list(out[len(pitches) :])


def sine_cosine(numbers, points):
    ratio = 1.0 / points
    rest = numbers - jnp.round(numbers * ratio) * points
    x = rest * (math.pi * ratio)
    y = x * x
    sine = jnp.float32(-1.0 / 39916800.0)
    for factor in (1.0 / 362880.0, -1.0 / 5040.0, 1.0 / 120.0, -1.0 / 6.0, 1.0):
        sine = sine * y + jnp.float32(factor)
    sine = sine * x
    cosine = jnp.float32(1.0 / 479001600.0)
    for factor in (-1.0 / 3628800.0, 1.0 / 40320.0, -1.0 / 720.0, 1.0 / 24.0, -0.5, 1.0):
        cosine = cosine * y + jnp.float32(factor)
    return 1.0 - 2.0 * sine * sine, 2.0 * sine * cosine


def synthesis_kernel(
    sizes, points_ref, low_ref, head_ref, coeff_ref, pressure_ref, out_ref,
    turned_ref, angle_ref, left_ref, table_ref, first_ref, second_ref, height_ref, moved_ref,
):
    fld_count, wn_count, levels, wave_count, tall, units, slabs, band_tiles, first_turn, group, turn_pairs = sizes
    pairs = wave_count // 2
    pair_dev = pairs // wn_count
    rest = pair_dev - group
    head_rows = group * turn_pairs
    own, own_wn = lax.axis_index("fld"), lax.axis_index("wn")
    stratum_count = fld_count * levels
    fields = 2 * stratum_count + 1
    low = low_ref[...]
    low_even = low % 2 == 0
    mirror = wave_count - 1 - low
    waves = (jnp.where(low_even, low, mirror), jnp.where(low_even, mirror, low))

    for g in range(fld_count):
        blocks = []
        for d in range(g * wn_count, (g + 1) * wn_count):
            at = first_turn // 2 * group
            blocks += [head_ref[d, at : at + group, :], coeff_ref[d, :rest, :]]
        turned_ref[g] = turned_over(jnp.concatenate(blocks, 0))

    eight = lax.broadcasted_iota(jnp.int32, (8, 1), 0).astype(jnp.float32)
    lane = lax.broadcasted_iota(jnp.int32, (8, lanes), 1)
    spot = lax.broadcasted_iota(jnp.int32, (8, lanes), 0) * lanes + lane

    @pl.loop(0, 2)
    def _(t):
        tile = (first_turn + t) * fld_count + jnp.where(t == 0, own, fld_count - 1 - own)
        band = tile // band_tiles
        points = points_ref[tile * wn_count + own_wn]
        real_points = points.astype(jnp.float32)
        middle = points // 2
        unit_count = (middle + 1023) // 1024
        whole_rows = middle // lanes
        left_over = middle - whole_rows * lanes

        spin = []
        for parity in range(2):
            wave = waves[parity]
            number = wave.astype(jnp.float32)
            weight = jnp.where(wave == 0, 1.0, 2.0) * jnp.where(2 * wave < points, 1.0, 0.0)
            cosine, sine = sine_cosine(number * (eight * 128.0), real_points)
            spin.append((cosine * weight, sine * weight))
            base_cosine, base_sine = sine_cosine(number * eight, real_points)
            @pl.loop(0, unit_count)
            def _(u, parity=parity, base_cosine=base_cosine, base_sine=base_sine, number=number):
                for part in range(2):
                    steps = eight * 8.0 + (64.0 * part + 1024.0 * u.astype(jnp.float32))
                    turns = sine_cosine(number * steps, real_points)
                    for n in range(2):
                        angle_ref[parity, n, part * 8 : (part + 1) * 8, :] = turns[n]
                for step in range(0, 16, 2):
                    cosines, sines = [], []
                    for one in (step, step + 1):
                        turn_cosine = angle_ref[parity, 0, one : one + 1, :]
                        turn_sine = angle_ref[parity, 1, one : one + 1, :]
                        cosines.append(base_cosine * turn_cosine - base_sine * turn_sine)
                        sines.append(-(base_sine * turn_cosine + base_cosine * turn_sine))
                    at = pl.ds(pl.multiple_of(u * lanes + step * 8, 16), 16)
                    table_ref[parity, at, :pairs] = jnp.concatenate(cosines, 0).astype(jnp.bfloat16)
                    table_ref[parity, at, pairs:] = jnp.concatenate(sines, 0).astype(jnp.bfloat16)

        for side in range(2):
            for parity in range(2):
                cosine, sine = spin[parity]

                def twist(real, imag, cosine=cosine, sine=sine):
                    return real * cosine - imag * sine, real * sine + imag * cosine

                at = t * 4 * channel_rows + (parity * 2 + side) * channel_rows
                for field in range(0, fields, 2):
                    reals, imags = [], []
                    for one in (field, field + 1):
                        if one < fields - 1:
                            kind, stratum = one // stratum_count, one % stratum_count
                            row = at + (kind * levels + stratum % levels) * 2
                            real = turned_ref[stratum // levels, pl.ds(row, 1), :]
                            imag = turned_ref[stratum // levels, pl.ds(row + 1, 1), :]
                        elif one == fields - 1:
                            row = (parity * 2 + side) * 2
                            real = pressure_ref[t, pl.ds(row, 1), :]
                            imag = pressure_ref[t, pl.ds(row + 1, 1), :]
                        else:
                            reals.append(jnp.zeros((8, pairs), jnp.float32))
                            imags.append(jnp.zeros((8, pairs), jnp.float32))
                            continue
                        turned = twist(real, imag)
                        reals.append(turned[0])
                        imags.append(turned[1])
                    rows = slice(field * 8, (field + 2) * 8)
                    left_ref[side, parity, rows, :pairs] = jnp.concatenate(reals, 0).astype(jnp.bfloat16)
                    left_ref[side, parity, rows, pairs:] = jnp.concatenate(imags, 0).astype(jnp.bfloat16)

            source = band if side == 0 else wn_count - 1 - band
            for g in range(fld_count):
                height_ref[g * slabs : (g + 1) * slabs, :] = head_ref[
                    g * wn_count + source, head_rows : head_rows + slabs, :
                ]

            @pl.loop(0, unit_count)
            def _(u, side=side):
                sums = []
                for parity in range(2):
                    table = table_ref[parity, pl.ds(pl.multiple_of(u * lanes, lanes), lanes), :]
                    sums.append(
                        lax.dot_general(
                            left_ref[side, parity], table, (((1,), (1,)), ((), ())),
                            preferred_element_type=jnp.float32,
                        )
                    )
                first_ref[...] = sums[0] + sums[1]
                second_ref[...] = sums[0] - sums[1]
                begin = pl.multiple_of(u * 8, 8)
                for which, grid_ref in enumerate((first_ref, second_ref)):
                    if which == 0:
                        height = height_ref[pl.ds(begin, 8), :]
                    else:
                        back = lax.rem(lanes - left_over, lanes)
                        upper = pltpu.roll(height_ref[pl.ds(begin + whole_rows, 8), :], back, 1)
                        lower = pltpu.roll(height_ref[pl.ds(begin + whole_rows + 1, 8), :], back, 1)
                        height = jnp.where(lane < lanes - left_over, upper, lower)
                    warmth, moisture = estimate_column(grid_ref, height, stratum_count)
                    moved_ref[which, 0, pl.ds(32 + begin, 8), :] = warmth
                    moved_ref[which, 1, pl.ds(32 + begin, 8), :] = moisture

            for which in range(2):
                for tile in range(tall // 8):
                    place = spot + tile * 1024
                    near = moved_ref[0, which, 32 + tile * 8 : 40 + tile * 8, :] if tile < 3 else 0.0
                    start = 32 + tile * 8 - whole_rows
                    ahead = pltpu.roll(moved_ref[1, which, pl.ds(start, 8), :], left_over, 1)
                    behind = pltpu.roll(moved_ref[1, which, pl.ds(start - 1, 8), :], left_over, 1)
                    far = jnp.where(lane >= left_over, ahead, behind)
                    value = jnp.where(place < middle, near, far)
                    out_ref[t, side, which, tile * 8 : (tile + 1) * 8, :] = jnp.where(
                        place < points, value, 0.0
                    )


def estimate_column(grid_ref, height, stratum_count):
    def field(n):
        return grid_ref[n * 8 : (n + 1) * 8, :]

    kelvin = 288.0 + 12.0 * field(0)
    vapour = 0.008 + 0.002 * field(stratum_count)
    weighted = kelvin * (1.0 + 0.608 * vapour)
    level_height = thickness_scale * weighted
    kelvin_sum, vapour_sum, mixing_sum = kelvin, vapour, jnp.ones_like(kelvin)
    for k in range(1, stratum_count):
        next_kelvin = 288.0 + 12.0 * field(k)
        next_vapour = 0.008 + 0.002 * field(stratum_count + k)
        next_weighted = next_kelvin * (1.0 + 0.608 * next_vapour)
        thickness = (0.5 * thickness_scale) * (weighted + next_weighted)
        mixing = jnp.clip((height - level_height) / thickness, 0.0, 1.0)
        kelvin_sum = kelvin_sum + mixing * (next_kelvin - kelvin)
        vapour_sum = vapour_sum + mixing * (next_vapour - vapour)
        mixing_sum = mixing_sum + mixing
        level_height = level_height + thickness
        kelvin, vapour, weighted = next_kelvin, next_vapour, next_weighted
    log_pressure = math.log(100000.0) + 0.15 * field(2 * stratum_count) - log_step * mixing_sum
    exponent = 17.67 * (kelvin_sum - 273.15) / (kelvin_sum - 29.65)
    saturation = 611.2 * jnp.exp(exponent)
    return (
        (kelvin_sum - 288.0) * (1.0 / 12.0),
        vapour_sum * jnp.exp(log_pressure) / (0.622 * saturation),
    )


def synthesize(
    points, low_row, head, coeffs, pressure, levels, fld_count, slabs, band_tiles, first_turn, group, turn_pairs
):
    wn_count = coeffs.shape[0] // fld_count
    pairs = low_row.shape[1]
    wave_count = 2 * pairs
    tall = -(-fld_count * slabs // 8) * 8
    units = -(-fld_count * slabs * lanes // 2048)
    fields = 2 * fld_count * levels + 1
    rows = -(-fields // 2) * 16
    sizes = (fld_count, wn_count, levels, wave_count, tall, units, slabs, band_tiles, first_turn, group, turn_pairs)
    return pl.pallas_call(
        functools.partial(synthesis_kernel, sizes),
        in_specs=[pl.BlockSpec(memory_space=pltpu.SMEM)]
        + [pl.BlockSpec(memory_space=pltpu.VMEM)] * 4,
        out_specs=pl.BlockSpec(memory_space=pltpu.VMEM),
        out_shape=jax.ShapeDtypeStruct((2, 2, 2, tall, lanes), jnp.float32),
        scratch_shapes=[
            pltpu.VMEM((fld_count, lanes, pairs), jnp.float32),
            pltpu.VMEM((2, 2, 16, pairs), jnp.float32),
            pltpu.VMEM((2, 2, rows, wave_count), jnp.bfloat16),
            pltpu.VMEM((2, units * lanes, wave_count), jnp.bfloat16),
            pltpu.VMEM((rows, lanes), jnp.float32),
            pltpu.VMEM((rows, lanes), jnp.float32),
            pltpu.VMEM((tall + 32, lanes), jnp.float32),
            pltpu.VMEM((2, 2, 32 + tall + 32, lanes), jnp.float32),
        ],
        compiler_params=pltpu.CompilerParams(vmem_limit_bytes=48 * 1024 * 1024),
        cost_estimate=pl.CostEstimate(
            flops=8 * rows * wave_count * units * lanes, bytes_accessed=coeffs.size * 8, transcendentals=0
        ),
        name="synthesis",
    )(points, low_row, head, coeffs, pressure)


def shards(spec_tq, spec_sp, legendre, low_wavenumber, lon_points, requested_elevation):
    wn_count = lax.axis_size("wn")
    fld_count = lax.axis_size("fld")
    pair_dev, _, levels, _, packed = spec_tq.shape
    half_rows = legendre.shape[1]
    pairs = low_wavenumber.shape[0]
    band_rows, tile_width = requested_elevation.shape
    tile_count = half_rows // wn_count
    turns = tile_count // fld_count
    band_tiles = band_rows // wn_count
    wn_index = lax.axis_index("wn")
    fld_index = lax.axis_index("fld")
    everyone = ("fld", "wn")
    devices = fld_count * wn_count
    slabs = tile_width // lanes
    out_tall = slabs * fld_count

    group = 16 if pair_dev % 16 == 0 else 8

    def exchange(block):
        return lax.all_to_all(block, everyone, split_axis=0, concat_axis=0, tiled=True)

    arguments = (spec_tq, spec_sp, legendre, low_wavenumber, requested_elevation, fld_count, wn_count, group)
    first, known = legendre_sums(*arguments, None)
    head = exchange(first)
    sent = legendre_sums(*arguments, known)
    later, head = lax.optimization_barrier((sent[-1], head))
    carrier = exchange(later)
    arrived = [None] * (turns // 2)
    arrived[-1] = carrier
    for n in range(turns // 2 - 1):
        later, carrier = lax.optimization_barrier((sent[n], carrier))
        arrived[n] = exchange(later)

    share = pair_dev // fld_count
    share_rows = -(-share // 4)
    rest = pair_dev - group
    pressure = carrier[:, rest : rest + share_rows]
    pressure = pressure.reshape(fld_count, wn_count, share_rows, 4, 4, 8)[:, :, :, :turns]
    pressure = jnp.transpose(pressure, (3, 5, 1, 0, 2, 4))
    pressure = pressure.reshape(turns, 8, wn_count, fld_count, share_rows * 4)[..., :share]
    pressure = pressure.reshape(turns, 8, pairs)

    low_row = low_wavenumber.reshape(1, pairs)
    results = [None] * (turns // 2)
    for n in reversed(range(turns // 2)):
        results[n] = synthesize(
            lon_points, low_row, head, arrived[n], pressure[2 * n : 2 * n + 2], levels,
            fld_count, slabs, band_tiles, 2 * n, group, turns // 2,
        )

    north = wn_index < wn_count // 2
    band = jnp.where(north, wn_index, wn_count - 1 - wn_index)
    turn = band * band_tiles // fld_count
    own_row = jnp.arange(band_rows, dtype=jnp.int32)
    mirrored = jnp.where(north, own_row, band_rows - 1 - own_row)
    tile_in_turn = (band * band_tiles + mirrored // wn_count) % fld_count
    owner_for_row = (
        jnp.where(turn % 2 == 0, tile_in_turn, fld_count - 1 - tile_in_turn) * wn_count
        + mirrored % wn_count
    )
    result = jnp.concatenate(results, 0)[:, :, :, :out_tall]
    turn_of = [min(s, wn_count - 1 - s) * band_tiles // fld_count for s in range(wn_count)]
    side_of = [0 if s < wn_count // 2 else 1 for s in range(wn_count)]
    back = jnp.stack([result[t, side] for t, side in zip(turn_of, side_of)])
    back = back.reshape(wn_count, 2, fld_count, slabs, lanes)
    back = jnp.transpose(back, (2, 0, 1, 3, 4)).reshape(devices, 2, tile_width)
    back = lax.all_to_all(back, everyone, split_axis=0, concat_axis=0, tiled=True)
    back = jnp.take(back, owner_for_row, axis=0)
    return back[:, 0], back[:, 1]


def solution(mesh):
    in_specs = (
        P("wn", None, "fld", None, None),
        P("wn", None, None),
        P("wn", None, None),
        P(),
        P(),
        P("wn", "fld"),
    )
    out_specs = (P("wn", "fld"), P("wn", "fld"))
    return jax.shard_map(shards, mesh=mesh, in_specs=in_specs, out_specs=out_specs, check_vma=False)
```

time: 1180 us -> 128 us (0.11); the launches traced: 1160 us -> 127 us
  other arithmetic: 528 us -> 0.28 us
  local copies, waits for them, and re-layouts: 310 us -> 14.6 us
  waiting for transfers between devices: 153 us -> 19.4 us
  matrix products: 81.2 us -> 0 us
  loops' own time: 80.2 us -> 0 us
  Pallas kernels: 0 us -> 44.8 us
  blocking collectives: 0 us -> 34.3 us
    cos x32 -> x0, other arithmetic: 276 us -> none  [twisted(): cosine = jnp.cos(phase)[:, None, :]]
    another operation x66 -> x0, other arithmetic: 177 us -> none
    dynamic_update_slice x32 -> x0, local copies, waits for them, and re-layouts: 141 us -> none  [synthesize_rows(): result = lax.map(one_row, (coeffs, grid_point_rows))]
    all_to_all x2 -> x3, waiting for transfers between devices: 153 us -> 19.4 us  [the longest x1 12.5 us: shards(): lax.all_to_all(back, everyone, split_axis=0, concat_axis=0, tiled=True)]
    dot_general x33 -> x0, matrix products: 81.2 us -> none  [the longest x32 57.7 us: contract(): jnp.einsum('qfj,jp->fpq', twisted(coeffs, wave_line, points), wave_table(...]
    another operation x1 -> x0, loops' own time: 80.2 us -> none  [synthesize_rows(): result = lax.map(one_row, (coeffs, grid_point_rows))]
    unnamed x16 -> x12, local copies, waits for them, and re-layouts: 63.1 us -> 0.86 us
    pallas_call x0 -> x4, Pallas kernels: none -> 44.8 us  [the longest x2 25.8 us: legendre_sums(): pl.pallas_call(functools.partial(legendre_kernel, sizes), grid_spec=pltpu...]
  transfers between devices with their start and end apart: 2 -> 3, of which waited for: 2 -> 3; matrix products, arithmetic and copies ran while one was open for 1% -> 9% of each run, Pallas kernels for 0% -> 23%
where the time goes in v1:
time: 128 us; the launch traced here: 127 us
  Pallas kernels  44.8 us (35%)
  blocking collectives  34.3 us (27%)
  waiting for transfers between devices  19.4 us (15%)
  local copies, waits for them, and re-layouts  14.6 us (11%)
  starting transfers between devices  12.6 us (10%)
    all_to_all x1, blocking collectives, exchange(): lax.all_to_all(block, everyone, split_axis=0, concat_axis=0, tiled=True)  34.3 us
    pallas_call x2, Pallas kernels, legendre_sums(): pl.pallas_call(functools.partial(legendre_kernel, sizes), grid_spec=pltpu...  25.8 us
    pallas_call x2, Pallas kernels, synthesize(): pl.pallas_call(functools.partial(synthesis_kernel, sizes), in_specs=[pl.B...  19 us
    all_to_all x1, waiting for transfers between devices, shards(): lax.all_to_all(back, everyone, split_axis=0, concat_axis=0, tiled=True)  12.5 us
    all_to_all x2, starting transfers between devices, exchange(): lax.all_to_all(block, everyone, split_axis=0, concat_axis=0, tiled=True)  9.84 us
    slice x5, local copies, waits for them, and re-layouts, shards(): pressure[2 * n:2 * n + 2]  8.01 us
    all_to_all x2, waiting for transfers between devices, exchange(): lax.all_to_all(block, everyone, split_axis=0, concat_axis=0, tiled=True)  6.9 us
    all_to_all x1, starting transfers between devices, shards(): lax.all_to_all(back, everyone, split_axis=0, concat_axis=0, tiled=True)  2.78 us
  transfers between devices with their start and end apart: 3, of which 3 were waited for; matrix products, arithmetic and copies ran while one was open for 9% of the time, Pallas kernels for 23%

profile of v1, /device:TPU:0, one launch (start us, length us, event | category | flops | bytes accessed | tf_op | source)
XLA Modules:
  0.0 126.9 jit_solution(15558945458402761235)
XLA Ops:
  0.6 0.6 broadcast_in_dim.14.known_ref
  1.2 8.0 %legendre_head.1 = (f32[1536,128]{1,0:T(8,128)}, f32[128,128]{1,0:T(8,128)}) custom-call(s32[640]{0:T(1024)} %low_ref.3, bf16[80,2,4,2,1281]{4,3,2,1,0:T(2,128)(2,1)} %spec_ref.3, bf16[80,2,1281]{2,1,0:T(2,128)(2,1)} %sp_ref.3, bf16[1281,80,128]{2,1,0:T(8,128)(2,1)} %bitcast.24, s32[32,1408]{1,0:T(8,128)} %elevation_ref.3, f32[8,128]{1,0:T(8,128)} %broadcast_in_dim.14.known_ref), custom_call_target="tpu_custom_call" | custom-call | flops 419430400 | bytes 5246976 | tf_op jit(solution)/shard_map/legendre_head/pallas_call | solution.py:242
  9.2 6.9 %all-to-all-start = ((f32[32,48,128]{2,1,0:T(8,128)}), f32[32,48,128]{2,1,0:T(8,128)S(1)}, u32[]{:S(2)}, u32[]{:S(2)}) async-start(f32[32,48,128]{2,1,0:T(8,128)} %bitcast.31), calls=%async_computation | async-start | bytes 1572864 | tf_op jit(solution)/shard_map/all_to_all | solution.py:517
  16.1 17.8 %legendre_rest.1 = (f32[2048,128]{1,0:T(8,128)}, f32[2304,128]{1,0:T(8,128)}) custom-call(s32[640]{0:T(1024)} %low_ref.3, bf16[80,2,4,2,1281]{4,3,2,1,0:T(2,128)(2,1)} %spec_ref.3, bf16[80,2,1281]{2,1,0:T(2,128)(2,1)} %sp_ref.3, bf16[1281,80,128]{2,1,0:T(8,128)(2,1)} %bitcast.25, s32[32,1408]{1,0:T(8,128)} %elevation_ref.3, ...), custom_call_target="tpu_custom_call" | custom-call | flops 1677721600 | bytes 20987904 | tf_op jit(solution)/shard_map/legendre_rest/pallas_call | solution.py:242
  33.9 2.8 %all-to-all-done.head_ref = f32[32,48,128]{2,1,0:T(8,128)S(1)} async-done(((f32[32,48,128]{2,1,0:T(8,128)}), f32[32,48,128]{2,1,0:T(8,128)S(1)}, u32[]{:S(2)}, u32[]{:S(2)}) %all-to-all-start) | async-done | bytes 786464 | tf_op jit(solution)/shard_map/all_to_all | solution.py:517
  36.7 34.3 %all_to_all.20.coeff_ref = f32[32,72,128]{2,1,0:T(8,128)S(1)} all-to-all(f32[32,72,128]{2,1,0:T(8,128)} %bitcast.29), channel_id=1, replica_groups=mesh['fld'=4,'wn'=8] {'fld','wn'}, dimensions={0} | all-to-all | bytes 2359296 | tf_op jit(solution)/shard_map/all_to_all | solution.py:517
  71.0 0.0 copy-start.1
  71.0 3.0 %all-to-all-start.2 = ((f32[32,64,128]{2,1,0:T(8,128)}), f32[32,64,128]{2,1,0:T(8,128)S(1)}, u32[]{:S(2)}, u32[]{:S(2)}) async-start(f32[32,64,128]{2,1,0:T(8,128)} %bitcast.30), calls=%async_computation.2 | async-start | bytes 2097152 | tf_op jit(solution)/shard_map/all_to_all | solution.py:517
  74.0 0.0 copy-done.1
  74.0 2.7 %reshape.184 = f32[4,8,5,4,4,8]{5,4,3,1,0,2:T(4,128)} reshape(f32[32,5,128]{2,0,1:T(8,128)S(1)} %copy.9) | data formatting | bytes 163840 | tf_op jit(solution)/shard_map/reshape | solution.py:535
  76.7 2.5 %fusion.5 = (f32[2,8,8,4,5,4]{1,5,0,2,3,4:T(4,128)}, f32[2,8,8,4,5,4]{1,5,0,2,3,4:T(4,128)S(1)}) fusion(f32[4,8,8,4,5,4]{1,5,0,2,3,4:T(4,128)} %bitcast.26), kind=kLoop, calls=%fused_computation.41 | loop fusion | bytes 163840 | tf_op jit(solution)/shard_map/slice | solution.py:544
  79.2 0.9 copy.10
  80.1 0.0 copy-start
  80.1 1.3 %copy.11.pressure_ref = f32[2,8,640]{2,1,0:T(8,128)S(1)} copy(f32[2,8,640]{1,2,0:T(8,128)} %bitcast.27) | data formatting | bytes 81920 | tf_op jit(solution)/shard_map/slice | solution.py:544
  81.4 2.0 %copy.14 = f32[2,8,8,4,5,4]{1,5,4,3,2,0:T(4,128)} copy(f32[2,8,8,4,5,4]{1,5,0,2,3,4:T(4,128)} %get-tuple-element.18) | data formatting | bytes 81920 | tf_op jit(solution)/shard_map/slice | solution.py:544
  83.4 1.3 %copy.15.pressure_ref = f32[2,8,640]{2,1,0:T(8,128)S(1)} copy(f32[2,8,640]{1,2,0:T(8,128)} %bitcast.28) | data formatting | bytes 81920 | tf_op jit(solution)/shard_map/slice | solution.py:544
  84.7 0.0 copy-done
  84.7 11.1 %synthesis.3 = f32[2,2,2,48,128]{4,3,2,1,0:T(8,128)S(1)} custom-call(s32[128]{0:T(128)S(1)} %copy-done, s32[1,640]{1,0:T(1,128)S(1)} %reshape.180.low_ref, f32[32,48,128]{2,1,0:T(8,128)S(1)} %all-to-all-done.head_ref, f32[32,72,128]{2,1,0:T(8,128)S(1)} %all_to_all.20.coeff_ref, f32[2,8,640]{2,1,0:T(8,128)S(1)} %copy.15.pressure_ref), custom_call_target="tpu_custom_call" | custom-call | flops 1069547520 | bytes 2359296 | tf_op jit(solution)/shard_map/synthesis/pallas_call | solution.py:473
  96.0 4.1 %all-to-all-done.2.coeff_ref = f32[32,64,128]{2,1,0:T(8,128)S(1)} async-done(((f32[32,64,128]{2,1,0:T(8,128)}), f32[32,64,128]{2,1,0:T(8,128)S(1)}, u32[]{:S(2)}, u32[]{:S(2)}) %all-to-all-start.2) | async-done | bytes 1048608 | tf_op jit(solution)/shard_map/all_to_all | solution.py:517
  100.0 8.0 %synthesis.2 = f32[2,2,2,48,128]{4,3,2,1,0:T(8,128)S(1)} custom-call(s32[128]{0:T(128)S(1)} %copy-done, s32[1,640]{1,0:T(1,128)S(1)} %reshape.180.low_ref, f32[32,48,128]{2,1,0:T(8,128)S(1)} %all-to-all-done.head_ref, f32[32,64,128]{2,1,0:T(8,128)S(1)} %all-to-all-done.2.coeff_ref, f32[2,8,640]{2,1,0:T(8,128)S(1)} %copy.11.pressure_ref), custom_call_target="tpu_custom_call" | custom-call | flops 1069547520 | bytes 2097152 | tf_op jit(solution)/shard_map/synthesis/pallas_call | solution.py:473
  108.3 0.1 copy.24
  108.4 0.9 reshape.194
  109.3 2.8 %all-to-all-start.3 = ((f32[32,2,1408]{2,1,0:T(2,128)}), f32[32,2,1408]{2,1,0:T(2,128)S(1)}, u32[]{:S(2)}, u32[]{:S(2)}) async-start(f32[32,2,1408]{2,1,0:T(2,128)} %reshape.194), calls=%async_computation.3 | async-start | bytes 720896 | tf_op jit(solution)/shard_map/all_to_all | solution.py:564
  112.2 12.5 %all-to-all-done.3 = f32[32,2,1408]{2,1,0:T(2,128)S(1)} async-done(((f32[32,2,1408]{2,1,0:T(2,128)}), f32[32,2,1408]{2,1,0:T(2,128)S(1)}, u32[]{:S(2)}, u32[]{:S(2)}) %all-to-all-start.3) | async-done | bytes 360480 | tf_op jit(solution)/shard_map/all_to_all | solution.py:564
  124.7 0.9 gather_fusion
  125.6 0.2 broadcast_select_fusion
  125.9 0.3 fusion.6
  126.1 0.8 copy_bitcast_fusion
  (24 shorter events, 0.4 us)
Async XLA Ops:
  9.2 27.5 %all-to-all-start = ((f32[32,48,128]{2,1,0:T(8,128)}), f32[32,48,128]{2,1,0:T(8,128)S(1)}, u32[]{:S(2)}, u32[]{:S(2)}) async-start(f32[32,48,128]{2,1,0:T(8,128)} %bitcast.31), calls=%async_computation | async-start | bytes 1572864 | tf_op jit(solution)/shard_map/all_to_all | solution.py:517
  71.0 3.0 %copy-start.1 = (s32[640]{0:T(1024)S(1)}, s32[640]{0:T(1024)}, u32[]{:S(2)}) copy-start(s32[640]{0:T(1024)} %low_ref.3) | copy-start | bytes 7684
  71.0 29.0 %all-to-all-start.2 = ((f32[32,64,128]{2,1,0:T(8,128)}), f32[32,64,128]{2,1,0:T(8,128)S(1)}, u32[]{:S(2)}, u32[]{:S(2)}) async-start(f32[32,64,128]{2,1,0:T(8,128)} %bitcast.30), calls=%async_computation.2 | async-start | bytes 2097152 | tf_op jit(solution)/shard_map/all_to_all | solution.py:517
  80.1 4.6 %copy-start = (s32[128]{0:T(128)S(1)}, s32[128]{0:T(128)}, u32[]{:S(2)}) copy-start(s32[128]{0:T(128)} %points_ref.3) | copy-start | bytes 1540
  109.3 15.4 %all-to-all-start.3 = ((f32[32,2,1408]{2,1,0:T(2,128)}), f32[32,2,1408]{2,1,0:T(2,128)S(1)}, u32[]{:S(2)}, u32[]{:S(2)}) async-start(f32[32,2,1408]{2,1,0:T(2,128)} %reshape.194), calls=%async_computation.3 | async-start | bytes 720896 | tf_op jit(solution)/shard_map/all_to_all | solution.py:564

commit v2 on v1

--- a/solution.py
+++ b/solution.py
@@ -11,6 +11,7 @@
 lanes = 128
 depth = 256
 channel_rows = 16
+streams = 4
 near, far = 3, 25
 thickness_scale = 0.012 * 287.05 / 9.80665
 log_step = 0.012
@@ -33,15 +34,17 @@
 
 
 def legendre_kernel(
-    sizes, low_ref, spec_ref, sp_ref, plane_ref, elevation_ref, known_ref, *rest
+    sizes, low_ref, spec_ref, sp_ref, *rest
 ):
     fld_count, wn_count, pair_dev, group, last, levels, halves, turns, head, starts, pitches = sizes
+    plane_refs, tail_ref, extra_ref = rest[:streams], rest[streams], rest[streams + 1]
+    rest = rest[streams + 2 :]
     out_count = len(pitches) + (1 if head else 0)
     (*out_refs, matrix, total, even_rows, odd_rows, stage) = rest[: out_count + 5]
     sp_rows = out_refs.pop() if head else rest[-1]
     first_block = 0 if head else 1
     out_of = [0 if head else n for n in range(turns // 2)]
-    half, step = pl.program_id(0), pl.program_id(1)
+    half, step = pl.program_id(0), 0 if head else pl.program_id(1)
     block = step + first_block
     own, own_wn = lax.axis_index("fld"), lax.axis_index("wn")
     packed = last + 1
@@ -83,91 +86,102 @@
             rows = [even, even_swung * flip.astype(jnp.float32), pressure - even, swung - even_swung]
             matrix[i, main_rows:, :packed] = jnp.concatenate(rows * 2, 0).astype(jnp.bfloat16)
 
-    @pl.loop(0, group // 2)
-    def _(n):
-        build(2 * n)
-        build(2 * n + 1)
+    def build_all():
+        @pl.loop(0, group // 2)
+        def _(n):
+            build(2 * n)
+            build(2 * n + 1)
 
     chunks = last // depth
+    stream = last // streams
     pitch = group + 1
 
     def widen(begin, end, buffer):
         for k in range(begin, end):
-            rows = plane_ref[k].astype(jnp.float32)
+            rows = plane_refs[k // stream][k % stream].astype(jnp.float32)
             for n in range(group // 8):
                 at = n * depth * far + (k % depth) * far
                 buffer[pl.ds(at, 8, stride=near), :] = rows[8 * n : 8 * n + 8]
 
-    buffers = (even_rows, odd_rows)
-    widen(0, depth, buffers[0])
-    for chunk in range(chunks):
-        source, target = buffers[chunk % 2], buffers[(chunk + 1) % 2]
-        for i in range(group):
-            at = (i // 8) * depth * far + (i % 8) * near
-            plane = source[pl.ds(at, depth, stride=far), :].astype(jnp.bfloat16)
-            part = jnp.dot(
-                matrix[i, :, chunk * depth : (chunk + 1) * depth],
-                plane,
-                preferred_element_type=jnp.float32,
-            )
-            if chunk == 0:
-                total[i] = part
-            else:
-                total[i] += part
-            if chunk + 1 < chunks:
-                begin = (chunk + 1) * depth
-                widen(begin + depth * i // group, begin + depth * (i + 1) // group, target)
-
-    tail = plane_ref[last].astype(jnp.float32)
-    low_lanes = lax.broadcasted_iota(jnp.int32, (wn_count, lanes), 1) < lanes // 2
-    for first in range(0, group, 4):
-        four = []
-        for j in range(first, first + 4):
-            column = matrix[j, :, last : last + 1].astype(jnp.float32)
-            summed = total[j] + column * tail[j : j + 1]
-            four.append(summed[:main_rows])
-            at = ((half if head else block) * group + j) * 8
-            sp_rows[pl.ds(pl.multiple_of(at, 8), 8), :] = summed[main_rows : main_rows + 8]
-        quad = turned_over(jnp.concatenate(four, 0))
-        for i in (first, first + 2):
-            turned = quad[:, (i - first) * lanes // 2 :][:, :lanes]
-            here = [turned[b * wn_count : (b + 1) * wn_count] for b in range(tiles)]
-            moved = [pltpu.roll(tile, lanes // 2, 1) for tile in here]
-            for n in range(turns // 2):
-                for g in range(fld_count):
-                    if halves == 1:
-                        b, c = tile_of(2 * n, g, fld_count), tile_of(2 * n + 1, g, fld_count)
-                        both = (
-                            jnp.where(low_lanes, here[b], moved[c]),
-                            jnp.where(low_lanes, moved[b], here[c]),
-                        )
-                    else:
-                        c = fld_count - 1 - g
-                        both = (
-                            jnp.where(half == 0, here[g], moved[c]),
-                            jnp.where(half == 0, moved[g], here[c]),
-                        )
-                    for j in range(2):
-                        at = g * wn_count * pitch + i + j
-                        stage[n, pl.ds(at, wn_count, stride=pitch), :] = both[j]
-
-    for n in range(turns // 2):
-        out = out_refs[out_of[n]]
-        for d in range(dest):
-            rows = stage[n, d * pitch : d * pitch + group, :]
-            at = d * pitches[out_of[n]] + starts[n] + step * group
-            at = pl.ds(pl.multiple_of(at, 8), group)
-            if halves > 1:
-                lane = lax.broadcasted_iota(jnp.int32, (group, lanes), 1)
-                rows = jnp.where((lane < lanes // 2) & (half == 1), out[at, :], rows)
-            out[at, :] = rows
+    def plane_of(i, source):
+        at = (i // 8) * depth * far + (i % 8) * near
+        return source[pl.ds(at, depth, stride=far), :].astype(jnp.bfloat16)
+
+    def sum_all():
+        buffers = (even_rows, odd_rows)
+        widen(0, depth, buffers[0])
+        for chunk in range(chunks):
+            source, target = buffers[chunk % 2], buffers[(chunk + 1) % 2]
+            for i in range(group):
+                plane = plane_of(i, source)
+                part = jnp.dot(
+                    matrix[i, :, chunk * depth : (chunk + 1) * depth],
+                    plane,
+                    preferred_element_type=jnp.float32,
+                )
+                if chunk == 0:
+                    total[i] = part
+                else:
+                    total[i] += part
+                if chunk + 1 < chunks:
+                    begin = (chunk + 1) * depth
+                    widen(begin + depth * i // group, begin + depth * (i + 1) // group, target)
+
+    def finish():
+        tail = tail_ref[0].astype(jnp.float32)
+        low_lanes = lax.broadcasted_iota(jnp.int32, (wn_count, lanes), 1) < lanes // 2
+        for first in range(0, group, 4):
+            four = []
+            for j in range(first, first + 4):
+                column = matrix[j, :, last : last + 1].astype(jnp.float32)
+                summed = total[j] + column * tail[j : j + 1]
+                four.append(summed[:main_rows])
+                at = ((half if head else block) * group + j) * 8
+                sp_rows[pl.ds(pl.multiple_of(at, 8), 8), :] = summed[main_rows : main_rows + 8]
+            quad = turned_over(jnp.concatenate(four, 0))
+            for i in (first, first + 2):
+                turned = quad[:, (i - first) * lanes // 2 :][:, :lanes]
+                here = [turned[b * wn_count : (b + 1) * wn_count] for b in range(tiles)]
+                moved = [pltpu.roll(tile, lanes // 2, 1) for tile in here]
+                for n in range(turns // 2):
+                    for g in range(fld_count):
+                        if halves == 1:
+                            b, c = tile_of(2 * n, g, fld_count), tile_of(2 * n + 1, g, fld_count)
+                            both = (
+                                jnp.where(low_lanes, here[b], moved[c]),
+                                jnp.where(low_lanes, moved[b], here[c]),
+                            )
+                        else:
+                            c = fld_count - 1 - g
+                            both = (
+                                jnp.where(half == 0, here[g], moved[c]),
+                                jnp.where(half == 0, moved[g], here[c]),
+                            )
+                        for j in range(2):
+                            at = g * wn_count * pitch + i + j
+                            stage[n, pl.ds(at, wn_count, stride=pitch), :] = both[j]
+
+        for n in range(turns // 2):
+            out = out_refs[out_of[n]]
+            for d in range(dest):
+                rows = stage[n, d * pitch : d * pitch + group, :]
+                at = d * pitches[out_of[n]] + starts[n] + step * group
+                at = pl.ds(pl.multiple_of(at, 8), group)
+                if halves > 1:
+                    lane = lax.broadcasted_iota(jnp.int32, (group, lanes), 1)
+                    rows = jnp.where((lane < lanes // 2) & (half == 1), out[at, :], rows)
+                out[at, :] = rows
+
+    build_all()
+    sum_all()
+    finish()
 
     if head:
-        slabs = elevation_ref.shape[1] // lanes
-        band_rows = elevation_ref.shape[0]
+        slabs = extra_ref.shape[1] // lanes
+        band_rows = extra_ref.shape[0]
         band_tiles = band_rows // wn_count
 
-        @pl.when((half == 0) & (step == 0))
+        @pl.when(half == 0)
         def _():
             north = own_wn < wn_count // 2
             band = jnp.where(north, own_wn, wn_count - 1 - own_wn)
@@ -178,7 +192,7 @@
                 inside = jnp.clip(turn * fld_count + tile - band * band_tiles, 0, band_tiles - 1)
                 row = inside * wn_count + e
                 row = jnp.where(north, row, band_rows - 1 - row)
-                heights = elevation_ref[pl.ds(row, 1), :].astype(jnp.float32)
+                heights = extra_ref[pl.ds(row, 1), :].astype(jnp.float32)
                 for n in range(slabs):
                     at = d * pitches[0] + turns // 2 * group + n
                     out_refs[0][at : at + 1, :] = heights[:, n * lanes : (n + 1) * lanes]
@@ -187,7 +201,7 @@
 
     @pl.when(step == 0)
     def _():
-        sp_rows[: group * 8, :] = known_ref[pl.ds(pl.multiple_of(half * group * 8, 8), group * 8), :]
+        sp_rows[: group * 8, :] = extra_ref[pl.ds(pl.multiple_of(half * group * 8, 8), group * 8), :]
 
     out, row_pitch, carried = out_refs[-1], pitches[-1], pair_dev - group
 
@@ -224,20 +238,28 @@
     rows = 4 * channel_rows + 16
     width = -(-packed // lanes) * lanes
     if head:
-        starts, first_block, blocks = [n * group for n in range(turns // 2)], 0, 1
+        starts, blocks = [n * group for n in range(turns // 2)], 1
         slabs = elevation.shape[1] // lanes
         pitches = [-(-(group * turns // 2 + slabs) // 8) * 8]
-        known = jnp.zeros((8, lanes), jnp.float32)
     else:
-        starts, first_block, blocks = [0] * (turns // 2), 1, pair_dev // group - 1
-        extra = -(-(pair_dev // fld_count) // 4)
+        starts, blocks = [0] * (turns // 2), pair_dev // group - 1
+        share_rows = -(-(pair_dev // fld_count) // 4)
         pitches = [pair_dev - group] * (turns // 2)
-        pitches[-1] += -(-extra // 8) * 8
+        pitches[-1] += -(-share_rows // 8) * 8
     sizes = (
         fld_count, wn_count, pair_dev, group, last, levels, halves, turns, head, tuple(starts), tuple(pitches)
     )
     shapes = [(dest * pitch, lanes) for pitch in pitches]
     outs = shapes + ([(halves * group * 8, lanes)] if head else [])
+    extra = elevation if head else known
+
+    def pair_at(b):
+        return 0 if head else b + 1
+
+    plane_specs = [
+        pl.BlockSpec((last // streams, group, lanes), lambda h, b, *_, n=n: (n, pair_at(b), h))
+        for n in range(streams)
+    ]
     work = blocks * group * (rows * last * lanes * 2) * halves
     out = pl.pallas_call(
         functools.partial(legendre_kernel, sizes),
@@ -245,13 +267,11 @@
             num_scalar_prefetch=1,
             grid=(halves, blocks),
             in_specs=[
-                pl.BlockSpec(
-                    (group, 2, levels, 2, packed), lambda h, b, *_: (b + first_block, 0, 0, 0, 0)
-                ),
-                pl.BlockSpec((group, 2, packed), lambda h, b, *_: (b + first_block, 0, 0)),
-                pl.BlockSpec((packed, group, lanes), lambda h, b, *_: (0, b + first_block, h)),
-                pl.BlockSpec(elevation.shape, lambda h, b, *_: (0, 0)),
-                pl.BlockSpec(known.shape, lambda h, b, *_: (0, 0)),
+                pl.BlockSpec((group, 2, levels, 2, packed), lambda h, b, *_: (pair_at(b), 0, 0, 0, 0)),
+                pl.BlockSpec((group, 2, packed), lambda h, b, *_: (pair_at(b), 0, 0)),
+                *plane_specs,
+                pl.BlockSpec((1, group, lanes), lambda h, b, *_: (last, pair_at(b), h)),
+                pl.BlockSpec(extra.shape, lambda h, b, *_: (0, 0)),
             ],
             out_specs=[pl.BlockSpec(shape, lambda h, b, *_: (0, 0)) for shape in outs],
             scratch_shapes=[
@@ -269,7 +289,7 @@
             flops=work, bytes_accessed=blocks * group * packed * lanes * 2 * halves, transcendentals=0
         ),
         name="legendre_head" if head else "legendre_rest",
-    )(low_wavenumber, spec_tq, spec_sp, planes, elevation, known)
+    )(low_wavenumber, spec_tq, spec_sp, *[planes] * (streams + 1), extra)
     return [block.reshape(dest, -1, lanes) for block in out[: len(pitches)]] + list(out[len(pitches) :])
 
 
@@ -313,6 +333,8 @@
         turned_ref[g] = turned_over(jnp.concatenate(blocks, 0))
 
     eight = lax.broadcasted_iota(jnp.int32, (8, 1), 0).astype(jnp.float32)
+    four = (lax.broadcasted_iota(jnp.int32, (8, 1), 0) & 3).astype(jnp.float32)
+    northern = lax.broadcasted_iota(jnp.int32, (8, pairs), 0) < 4
     lane = lax.broadcasted_iota(jnp.int32, (8, lanes), 1)
     spot = lax.broadcasted_iota(jnp.int32, (8, lanes), 0) * lanes + lane
 
@@ -327,112 +349,119 @@
         whole_rows = middle // lanes
         left_over = middle - whole_rows * lanes
 
-        spin = []
+        for side in range(2):
+            source = band if side == 0 else wn_count - 1 - band
+            for g in range(fld_count):
+                height_ref[side, g * slabs : (g + 1) * slabs, :] = head_ref[
+                    g * wn_count + source, head_rows : head_rows + slabs, :
+                ]
+
         for parity in range(2):
             wave = waves[parity]
             number = wave.astype(jnp.float32)
             weight = jnp.where(wave == 0, 1.0, 2.0) * jnp.where(2 * wave < points, 1.0, 0.0)
-            cosine, sine = sine_cosine(number * (eight * 128.0), real_points)
-            spin.append((cosine * weight, sine * weight))
+            cosine, sine = sine_cosine(number * (four * 256.0), real_points)
+            cosine, sine = cosine * weight, sine * weight
             base_cosine, base_sine = sine_cosine(number * eight, real_points)
+
+            at = t * 4 * channel_rows + parity * 2 * channel_rows
+            for field in range(0, fields, 2):
+                reals, imags = [], []
+                for one in (field, field + 1):
+                    if one == fields:
+                        reals.append(jnp.zeros((8, pairs), jnp.float32))
+                        imags.append(jnp.zeros((8, pairs), jnp.float32))
+                        continue
+                    parts = []
+                    for imag in range(2):
+                        if one < fields - 1:
+                            kind, stratum = one // stratum_count, one % stratum_count
+                            row = at + (kind * levels + stratum % levels) * 2 + imag
+                            north = turned_ref[stratum // levels, pl.ds(row, 1), :]
+                            south = turned_ref[stratum // levels, pl.ds(row + channel_rows, 1), :]
+                        else:
+                            row = parity * 4 + imag
+                            north = pressure_ref[t, row : row + 1, :]
+                            south = pressure_ref[t, row + 2 : row + 3, :]
+                        parts.append(jnp.where(northern, north, south))
+                    reals.append(parts[0] * cosine - parts[1] * sine)
+                    imags.append(parts[0] * sine + parts[1] * cosine)
+                rows = slice(field * 8, (field + 2) * 8)
+                left_ref[parity, rows, :pairs] = jnp.concatenate(reals, 0).astype(jnp.bfloat16)
+                left_ref[parity, rows, pairs:] = jnp.concatenate(imags, 0).astype(jnp.bfloat16)
+
             @pl.loop(0, unit_count)
             def _(u, parity=parity, base_cosine=base_cosine, base_sine=base_sine, number=number):
-                for part in range(2):
+                for part in range(4):
                     steps = eight * 8.0 + (64.0 * part + 1024.0 * u.astype(jnp.float32))
                     turns = sine_cosine(number * steps, real_points)
                     for n in range(2):
                         angle_ref[parity, n, part * 8 : (part + 1) * 8, :] = turns[n]
-                for step in range(0, 16, 2):
+                for step in range(0, 32, 2):
                     cosines, sines = [], []
                     for one in (step, step + 1):
                         turn_cosine = angle_ref[parity, 0, one : one + 1, :]
                         turn_sine = angle_ref[parity, 1, one : one + 1, :]
                         cosines.append(base_cosine * turn_cosine - base_sine * turn_sine)
                         sines.append(-(base_sine * turn_cosine + base_cosine * turn_sine))
-                    at = pl.ds(pl.multiple_of(u * lanes + step * 8, 16), 16)
+                    at = pl.ds(pl.multiple_of(u * 2 * lanes + step * 8, 16), 16)
                     table_ref[parity, at, :pairs] = jnp.concatenate(cosines, 0).astype(jnp.bfloat16)
                     table_ref[parity, at, pairs:] = jnp.concatenate(sines, 0).astype(jnp.bfloat16)
 
-        for side in range(2):
+        @pl.loop(0, unit_count)
+        def _(u):
+            sums = []
             for parity in range(2):
-                cosine, sine = spin[parity]
-
-                def twist(real, imag, cosine=cosine, sine=sine):
-                    return real * cosine - imag * sine, real * sine + imag * cosine
-
-                at = t * 4 * channel_rows + (parity * 2 + side) * channel_rows
-                for field in range(0, fields, 2):
-                    reals, imags = [], []
-                    for one in (field, field + 1):
-                        if one < fields - 1:
-                            kind, stratum = one // stratum_count, one % stratum_count
-                            row = at + (kind * levels + stratum % levels) * 2
-                            real = turned_ref[stratum // levels, pl.ds(row, 1), :]
-                            imag = turned_ref[stratum // levels, pl.ds(row + 1, 1), :]
-                        elif one == fields - 1:
-                            row = (parity * 2 + side) * 2
-                            real = pressure_ref[t, pl.ds(row, 1), :]
-                            imag = pressure_ref[t, pl.ds(row + 1, 1), :]
-                        else:
-                            reals.append(jnp.zeros((8, pairs), jnp.float32))
-                            imags.append(jnp.zeros((8, pairs), jnp.float32))
-                            continue
-                        turned = twist(real, imag)
-                        reals.append(turned[0])
-                        imags.append(turned[1])
-                    rows = slice(field * 8, (field + 2) * 8)
-                    left_ref[side, parity, rows, :pairs] = jnp.concatenate(reals, 0).astype(jnp.bfloat16)
-                    left_ref[side, parity, rows, pairs:] = jnp.concatenate(imags, 0).astype(jnp.bfloat16)
-
-            source = band if side == 0 else wn_count - 1 - band
-            for g in range(fld_count):
-                height_ref[g * slabs : (g + 1) * slabs, :] = head_ref[
-                    g * wn_count + source, head_rows : head_rows + slabs, :
-                ]
-
-            @pl.loop(0, unit_count)
-            def _(u, side=side):
-                sums = []
-                for parity in range(2):
-                    table = table_ref[parity, pl.ds(pl.multiple_of(u * lanes, lanes), lanes), :]
-                    sums.append(
-                        lax.dot_general(
-                            left_ref[side, parity], table, (((1,), (1,)), ((), ())),
-                            preferred_element_type=jnp.float32,
-                        )
+                at = pl.ds(pl.multiple_of(u * 2 * lanes, lanes), 2 * lanes)
+                sums.append(
+                    lax.dot_general(
+                        left_ref[parity], table_ref[parity, at, :], (((1,), (1,)), ((), ())),
+                        preferred_element_type=jnp.float32,
                     )
-                first_ref[...] = sums[0] + sums[1]
-                second_ref[...] = sums[0] - sums[1]
-                begin = pl.multiple_of(u * 8, 8)
+                )
+            first_ref[...] = sums[0] + sums[1]
+            second_ref[...] = sums[0] - sums[1]
+            for column in range(2):
+                begin = u * 8 + column
+
+                def heights(start):
+                    sides = [height_ref[side, pl.ds(start, 4, stride=2), :] for side in range(2)]
+                    return jnp.concatenate(sides, 0)
+
                 for which, grid_ref in enumerate((first_ref, second_ref)):
                     if which == 0:
-                        height = height_ref[pl.ds(begin, 8), :]
+                        height = heights(begin)
                     else:
                         back = lax.rem(lanes - left_over, lanes)
-                        upper = pltpu.roll(height_ref[pl.ds(begin + whole_rows, 8), :], back, 1)
-                        lower = pltpu.roll(height_ref[pl.ds(begin + whole_rows + 1, 8), :], back, 1)
+                        upper = pltpu.roll(heights(begin + whole_rows), back, 1)
+                        lower = pltpu.roll(heights(begin + whole_rows + 1), back, 1)
                         height = jnp.where(lane < lanes - left_over, upper, lower)
-                    warmth, moisture = estimate_column(grid_ref, height, stratum_count)
-                    moved_ref[which, 0, pl.ds(32 + begin, 8), :] = warmth
-                    moved_ref[which, 1, pl.ds(32 + begin, 8), :] = moisture
-
+                    columns = slice(column * lanes, (column + 1) * lanes)
+                    results = estimate_column(grid_ref, columns, height, stratum_count)
+                    for n, value in enumerate(results):
+                        for side in range(2):
+                            at = pl.ds(32 + begin, 4, stride=2)
+                            moved_ref[which, n, side, at, :] = value[side * 4 : side * 4 + 4]
+
+        for side in range(2):
             for which in range(2):
-                for tile in range(tall // 8):
-                    place = spot + tile * 1024
-                    near = moved_ref[0, which, 32 + tile * 8 : 40 + tile * 8, :] if tile < 3 else 0.0
-                    start = 32 + tile * 8 - whole_rows
-                    ahead = pltpu.roll(moved_ref[1, which, pl.ds(start, 8), :], left_over, 1)
-                    behind = pltpu.roll(moved_ref[1, which, pl.ds(start - 1, 8), :], left_over, 1)
+                for tile_row in range(tall // 8):
+                    place = spot + tile_row * 1024
+                    begin = 32 + tile_row * 8
+                    near = moved_ref[0, which, side, begin : begin + 8, :] if tile_row < units else 0.0
+                    start = begin - whole_rows
+                    ahead = pltpu.roll(moved_ref[1, which, side, pl.ds(start, 8), :], left_over, 1)
+                    behind = pltpu.roll(moved_ref[1, which, side, pl.ds(start - 1, 8), :], left_over, 1)
                     far = jnp.where(lane >= left_over, ahead, behind)
                     value = jnp.where(place < middle, near, far)
-                    out_ref[t, side, which, tile * 8 : (tile + 1) * 8, :] = jnp.where(
+                    out_ref[t, side, which, tile_row * 8 : (tile_row + 1) * 8, :] = jnp.where(
                         place < points, value, 0.0
                     )
 
 
-def estimate_column(grid_ref, height, stratum_count):
+def estimate_column(grid_ref, columns, height, stratum_count):
     def field(n):
-        return grid_ref[n * 8 : (n + 1) * 8, :]
+        return grid_ref[n * 8 : (n + 1) * 8, columns]
 
     kelvin = 288.0 + 12.0 * field(0)
     vapour = 0.008 + 0.002 * field(stratum_count)
@@ -478,13 +507,13 @@
         out_shape=jax.ShapeDtypeStruct((2, 2, 2, tall, lanes), jnp.float32),
         scratch_shapes=[
             pltpu.VMEM((fld_count, lanes, pairs), jnp.float32),
-            pltpu.VMEM((2, 2, 16, pairs), jnp.float32),
-            pltpu.VMEM((2, 2, rows, wave_count), jnp.bfloat16),
-            pltpu.VMEM((2, units * lanes, wave_count), jnp.bfloat16),
-            pltpu.VMEM((rows, lanes), jnp.float32),
-            pltpu.VMEM((rows, lanes), jnp.float32),
-            pltpu.VMEM((tall + 32, lanes), jnp.float32),
-            pltpu.VMEM((2, 2, 32 + tall + 32, lanes), jnp.float32),
+            pltpu.VMEM((2, 2, 32, pairs), jnp.float32),
+            pltpu.VMEM((2, rows, wave_count), jnp.bfloat16),
+            pltpu.VMEM((2, units * 2 * lanes, wave_count), jnp.bfloat16),
+            pltpu.VMEM((rows, 2 * lanes), jnp.float32),
+            pltpu.VMEM((rows, 2 * lanes), jnp.float32),
+            pltpu.VMEM((2, tall + 32, lanes), jnp.float32),
+            pltpu.VMEM((2, 2, 2, 32 + tall + 32, lanes), jnp.float32),
         ],
         compiler_params=pltpu.CompilerParams(vmem_limit_bytes=48 * 1024 * 1024),
         cost_estimate=pl.CostEstimate(

time: 128 us -> 126 us (0.984)
  Pallas kernels: 44.8 us -> 42.9 us
    pallas_call x2, Pallas kernels: 19 us -> 16.8 us  [synthesize(): pl.pallas_call(functools.partial(synthesis_kernel, sizes), in_specs=[pl.B...]
  transfers between devices with their start and end apart: 3 -> 3, of which waited for: 3 -> 3; matrix products, arithmetic and copies ran while one was open for 9% -> 9% of each run, Pallas kernels for 23% -> 22%
where the time goes in v2:
time: 126 us; the launch traced here: 125 us
  Pallas kernels  42.9 us (34%)
  blocking collectives  34.3 us (27%)
  waiting for transfers between devices  20.4 us (16%)
  local copies, waits for them, and re-layouts  14 us (11%)
  starting transfers between devices  12.6 us (10%)
    all_to_all x1, blocking collectives, exchange(): lax.all_to_all(block, everyone, split_axis=0, concat_axis=0, tiled=True)  34.3 us
    pallas_call x2, Pallas kernels, legendre_sums(): pl.pallas_call(functools.partial(legendre_kernel, sizes), grid_spec=pltpu...  26.1 us
    pallas_call x2, Pallas kernels, synthesize(): pl.pallas_call(functools.partial(synthesis_kernel, sizes), in_specs=[pl.B...  16.8 us
    all_to_all x1, waiting for transfers between devices, shards(): lax.all_to_all(back, everyone, split_axis=0, concat_axis=0, tiled=True)  12.5 us
    all_to_all x2, starting transfers between devices, exchange(): lax.all_to_all(block, everyone, split_axis=0, concat_axis=0, tiled=True)  9.84 us
    slice x5, local copies, waits for them, and re-layouts, shards(): pressure[2 * n:2 * n + 2]  8.01 us
    all_to_all x2, waiting for transfers between devices, exchange(): lax.all_to_all(block, everyone, split_axis=0, concat_axis=0, tiled=True)  7.95 us
    all_to_all x1, starting transfers between devices, shards(): lax.all_to_all(back, everyone, split_axis=0, concat_axis=0, tiled=True)  2.77 us
  transfers between devices with their start and end apart: 3, of which 3 were waited for; matrix products, arithmetic and copies ran while one was open for 9% of the time, Pallas kernels for 22%

profile of v2, /device:TPU:0, one launch (start us, length us, event | category | flops | bytes accessed | tf_op | source)
XLA Modules:
  0.0 125.4 jit_solution(9447644208493829457)
XLA Ops:
  0.6 8.1 %legendre_head.1 = (f32[1536,128]{1,0:T(8,128)}, f32[128,128]{1,0:T(8,128)}) custom-call(s32[640]{0:T(1024)} %low_ref.3, bf16[80,2,4,2,1281]{4,3,2,1,0:T(2,128)(2,1)} %spec_ref.3, bf16[80,2,1281]{2,1,0:T(2,128)(2,1)} %sp_ref.3, bf16[1281,80,128]{2,1,0:T(8,128)(2,1)} %bitcast.24, bf16[1281,80,128]{2,1,0:T(8,128)(2,1)} %bitcast.25, ...), custom_call_target="tpu_custom_call" | custom-call | flops 419430400 | bytes 5246976 | tf_op jit(solution)/shard_map/legendre_head/pallas_call | solution.py:264
  8.7 6.9 %all-to-all-start = ((f32[32,48,128]{2,1,0:T(8,128)}), f32[32,48,128]{2,1,0:T(8,128)S(1)}, u32[]{:S(2)}, u32[]{:S(2)}) async-start(f32[32,48,128]{2,1,0:T(8,128)} %bitcast.39), calls=%async_computation | async-start | bytes 1572864 | tf_op jit(solution)/shard_map/all_to_all | solution.py:546
  15.6 18.0 %legendre_rest.1 = (f32[2048,128]{1,0:T(8,128)}, f32[2304,128]{1,0:T(8,128)}) custom-call(s32[640]{0:T(1024)} %low_ref.3, bf16[80,2,4,2,1281]{4,3,2,1,0:T(2,128)(2,1)} %spec_ref.3, bf16[80,2,1281]{2,1,0:T(2,128)(2,1)} %sp_ref.3, bf16[1281,80,128]{2,1,0:T(8,128)(2,1)} %bitcast.29, bf16[1281,80,128]{2,1,0:T(8,128)(2,1)} %bitcast.30, ...), custom_call_target="tpu_custom_call" | custom-call | flops 1677721600 | bytes 20987904 | tf_op jit(solution)/shard_map/legendre_rest/pallas_call | solution.py:264
  33.6 2.6 %all-to-all-done.head_ref = f32[32,48,128]{2,1,0:T(8,128)S(1)} async-done(((f32[32,48,128]{2,1,0:T(8,128)}), f32[32,48,128]{2,1,0:T(8,128)S(1)}, u32[]{:S(2)}, u32[]{:S(2)}) %all-to-all-start) | async-done | bytes 786464 | tf_op jit(solution)/shard_map/all_to_all | solution.py:546
  36.2 34.3 %all_to_all.20.coeff_ref = f32[32,72,128]{2,1,0:T(8,128)S(1)} all-to-all(f32[32,72,128]{2,1,0:T(8,128)} %bitcast.37), channel_id=1, replica_groups=mesh['fld'=4,'wn'=8] {'fld','wn'}, dimensions={0} | all-to-all | bytes 2359296 | tf_op jit(solution)/shard_map/all_to_all | solution.py:546
  70.5 0.0 copy-start.1
  70.5 3.0 %all-to-all-start.2 = ((f32[32,64,128]{2,1,0:T(8,128)}), f32[32,64,128]{2,1,0:T(8,128)S(1)}, u32[]{:S(2)}, u32[]{:S(2)}) async-start(f32[32,64,128]{2,1,0:T(8,128)} %bitcast.38), calls=%async_computation.2 | async-start | bytes 2097152 | tf_op jit(solution)/shard_map/all_to_all | solution.py:546
  73.5 0.0 copy-done.1
  73.5 2.7 %reshape.184 = f32[4,8,5,4,4,8]{5,4,3,1,0,2:T(4,128)} reshape(f32[32,5,128]{2,0,1:T(8,128)S(1)} %copy.9) | data formatting | bytes 163840 | tf_op jit(solution)/shard_map/reshape | solution.py:564
  76.2 2.5 %fusion.5 = (f32[2,8,8,4,5,4]{1,5,0,2,3,4:T(4,128)}, f32[2,8,8,4,5,4]{1,5,0,2,3,4:T(4,128)S(1)}) fusion(f32[4,8,8,4,5,4]{1,5,0,2,3,4:T(4,128)} %bitcast.34), kind=kLoop, calls=%fused_computation.41 | loop fusion | bytes 163840 | tf_op jit(solution)/shard_map/slice | solution.py:573
  78.6 0.9 copy.10
  79.6 0.0 copy-start
  79.6 1.3 %copy.11.pressure_ref = f32[2,8,640]{2,1,0:T(8,128)S(1)} copy(f32[2,8,640]{1,2,0:T(8,128)} %bitcast.35) | data formatting | bytes 81920 | tf_op jit(solution)/shard_map/slice | solution.py:573
  80.9 2.0 %copy.14 = f32[2,8,8,4,5,4]{1,5,4,3,2,0:T(4,128)} copy(f32[2,8,8,4,5,4]{1,5,0,2,3,4:T(4,128)} %get-tuple-element.18) | data formatting | bytes 81920 | tf_op jit(solution)/shard_map/slice | solution.py:573
  82.9 1.3 %copy.15.pressure_ref = f32[2,8,640]{2,1,0:T(8,128)S(1)} copy(f32[2,8,640]{1,2,0:T(8,128)} %bitcast.36) | data formatting | bytes 81920 | tf_op jit(solution)/shard_map/slice | solution.py:573
  84.2 0.0 copy-done
  84.2 9.8 %synthesis.3 = f32[2,2,2,48,128]{4,3,2,1,0:T(8,128)S(1)} custom-call(s32[128]{0:T(128)S(1)} %copy-done, s32[1,640]{1,0:T(1,128)S(1)} %reshape.180.low_ref, f32[32,48,128]{2,1,0:T(8,128)S(1)} %all-to-all-done.head_ref, f32[32,72,128]{2,1,0:T(8,128)S(1)} %all_to_all.20.coeff_ref, f32[2,8,640]{2,1,0:T(8,128)S(1)} %copy.15.pressure_ref), custom_call_target="tpu_custom_call" | custom-call | flops 1069547520 | bytes 2359296 | tf_op jit(solution)/shard_map/synthesis/pallas_call | solution.py:502
  94.2 5.3 %all-to-all-done.2.coeff_ref = f32[32,64,128]{2,1,0:T(8,128)S(1)} async-done(((f32[32,64,128]{2,1,0:T(8,128)}), f32[32,64,128]{2,1,0:T(8,128)S(1)}, u32[]{:S(2)}, u32[]{:S(2)}) %all-to-all-start.2) | async-done | bytes 1048608 | tf_op jit(solution)/shard_map/all_to_all | solution.py:546
  99.5 7.0 %synthesis.2 = f32[2,2,2,48,128]{4,3,2,1,0:T(8,128)S(1)} custom-call(s32[128]{0:T(128)S(1)} %copy-done, s32[1,640]{1,0:T(1,128)S(1)} %reshape.180.low_ref, f32[32,48,128]{2,1,0:T(8,128)S(1)} %all-to-all-done.head_ref, f32[32,64,128]{2,1,0:T(8,128)S(1)} %all-to-all-done.2.coeff_ref, f32[2,8,640]{2,1,0:T(8,128)S(1)} %copy.11.pressure_ref), custom_call_target="tpu_custom_call" | custom-call | flops 1069547520 | bytes 2097152 | tf_op jit(solution)/shard_map/synthesis/pallas_call | solution.py:502
  106.9 0.1 copy.24
  106.9 0.9 reshape.194
  107.9 2.8 %all-to-all-start.3 = ((f32[32,2,1408]{2,1,0:T(2,128)}), f32[32,2,1408]{2,1,0:T(2,128)S(1)}, u32[]{:S(2)}, u32[]{:S(2)}) async-start(f32[32,2,1408]{2,1,0:T(2,128)} %reshape.194), calls=%async_computation.3 | async-start | bytes 720896 | tf_op jit(solution)/shard_map/all_to_all | solution.py:593
  110.7 12.5 %all-to-all-done.3 = f32[32,2,1408]{2,1,0:T(2,128)S(1)} async-done(((f32[32,2,1408]{2,1,0:T(2,128)}), f32[32,2,1408]{2,1,0:T(2,128)S(1)}, u32[]{:S(2)}, u32[]{:S(2)}) %all-to-all-start.3) | async-done | bytes 360480 | tf_op jit(solution)/shard_map/all_to_all | solution.py:593
  123.2 0.9 gather_fusion
  124.2 0.2 broadcast_select_fusion
  124.4 0.3 fusion.6
  124.7 0.8 copy_bitcast_fusion
  (24 shorter events, 0.4 us)
Async XLA Ops:
  8.7 27.5 %all-to-all-start = ((f32[32,48,128]{2,1,0:T(8,128)}), f32[32,48,128]{2,1,0:T(8,128)S(1)}, u32[]{:S(2)}, u32[]{:S(2)}) async-start(f32[32,48,128]{2,1,0:T(8,128)} %bitcast.39), calls=%async_computation | async-start | bytes 1572864 | tf_op jit(solution)/shard_map/all_to_all | solution.py:546
  70.5 3.0 %copy-start.1 = (s32[640]{0:T(1024)S(1)}, s32[640]{0:T(1024)}, u32[]{:S(2)}) copy-start(s32[640]{0:T(1024)} %low_ref.3) | copy-start | bytes 7684
  70.5 29.0 %all-to-all-start.2 = ((f32[32,64,128]{2,1,0:T(8,128)}), f32[32,64,128]{2,1,0:T(8,128)S(1)}, u32[]{:S(2)}, u32[]{:S(2)}) async-start(f32[32,64,128]{2,1,0:T(8,128)} %bitcast.38), calls=%async_computation.2 | async-start | bytes 2097152 | tf_op jit(solution)/shard_map/all_to_all | solution.py:546
  79.6 4.6 %copy-start = (s32[128]{0:T(128)S(1)}, s32[128]{0:T(128)}, u32[]{:S(2)}) copy-start(s32[128]{0:T(128)} %points_ref.3) | copy-start | bytes 1540
  107.9 15.4 %all-to-all-start.3 = ((f32[32,2,1408]{2,1,0:T(2,128)}), f32[32,2,1408]{2,1,0:T(2,128)S(1)}, u32[]{:S(2)}, u32[]{:S(2)}) async-start(f32[32,2,1408]{2,1,0:T(2,128)} %reshape.194), calls=%async_computation.3 | async-start | bytes 720896 | tf_op jit(solution)/shard_map/all_to_all | solution.py:593
